TPU v7x, 512 devices: a whole 4x8x8 slice. The times are simulated.
512 devices in a mesh: row: 16 (over y, x_hi), col: 32 (over x_lo, z, core).
Axes of the slice: x: 4 (x_hi: 2, x_lo: 2; x = x_hi * 2 + x_lo), y: 8, z: 8, core: 2. Of those that a mesh axis runs over, the one named last changes fastest.
Arguments:
- integrals: bfloat16 [800, 800, 640], P('row', 'col'), may hold values from -0.625 to 0.625
- amplitudes: bfloat16 [1024, 640], P('row', 'col'), may hold values from -6 to 6
- virt_irrep: int32 [800], replicated, may hold values from 0 to 7, as said below
- pair_irrep: int32 [640], replicated, may hold values from 0 to 7, as said below
- virt_energy: float32 [800], replicated, may hold values from 0.3 to 4
- occ_energy: float32 [32], replicated, may hold values from -2 to -0.3
Outputs:
- update: bfloat16 [800, 800, 1024], P('row', 'col')
Inputs may be any that keep to these rules, and one draw needn't show every extreme that they name: `virt_irrep`: labels never fall along the index; each of the 8 labels covers one contiguous run of at least 66 orbitals. `pair_irrep`: labels never fall along the index; each of the 8 labels covers one contiguous run of at least 53 pairs.
All inputs are finite; a program needn't handle non-finite values.
Results may differ from a plain program's by a relative error of at most 0.0049.
Values may be sent and summed in bfloat16 or wider, within the bound.
A program may use at most 64 MiB of HBM per device.

v0:
```python
import jax
import jax.numpy as jnp
from jax import lax
from jax.sharding import PartitionSpec as P


def pair_swapper(occupied):
    pairs = occupied * occupied
    source = jnp.arange(pairs, dtype=jnp.int32)
    target = source % occupied * occupied + source // occupied
    return (source[:, None] == target[None, :]).astype(jnp.bfloat16)


def per_device(integrals, amplitudes, virt_irrep, pair_irrep, virt_energy, occ_energy):
    tile_a, tile_b, slab = integrals.shape
    occupied = occ_energy.shape[0]
    pairs = occupied * occupied
    row_at = lax.axis_index("row")
    col_at = lax.axis_index("col")
    labels_a = lax.dynamic_slice_in_dim(virt_irrep, row_at * tile_a, tile_a, 0)
    labels_b = lax.dynamic_slice_in_dim(virt_irrep, col_at * tile_b, tile_b, 0)
    keep = (
        jnp.bitwise_xor(labels_a[:, None, None], labels_b[None, :, None])
        == pair_irrep[None, None, :]
    )
    masked = jnp.where(keep, integrals, jnp.zeros((), integrals.dtype))
    flat = masked.reshape(tile_a * tile_b, slab)
    swapper = pair_swapper(occupied)
    all_pairs = lax.all_gather(amplitudes, "row", axis=0, tiled=True)
    totals = lax.dot_general(
        flat,
        lax.all_gather(all_pairs, "col", axis=1, tiled=True),
        (((1,), (1,)), ((), ())),
        preferred_element_type=jnp.float32,
    )
    rounded = totals.astype(jnp.bfloat16)
    ladder = rounded.reshape(tile_a, tile_b, pairs)
    first_move = lax.all_to_all(ladder, "row", split_axis=2, concat_axis=0, tiled=True)
    second_move = lax.all_to_all(first_move, "col", split_axis=0, concat_axis=1, tiled=True)
    third_move = lax.all_to_all(second_move, "row", split_axis=1, concat_axis=2, tiled=True)
    other = jnp.einsum("bap,pq->abq", third_move, swapper, preferred_element_type=jnp.float32)
    energy_a = lax.dynamic_slice_in_dim(virt_energy, row_at * tile_a, tile_a, 0)
    energy_b = lax.dynamic_slice_in_dim(virt_energy, col_at * tile_b, tile_b, 0)
    pair_energy = (occ_energy[:, None] + occ_energy[None, :]).reshape(pairs)
    denom = energy_a[:, None, None] + energy_b[None, :, None] - pair_energy[None, None, :]
    return ((ladder.astype(jnp.float32) + other) / denom).astype(jnp.bfloat16)


def solution(mesh):
    return jax.shard_map(
        per_device,
        mesh=mesh,
        in_specs=(P("row", "col", None), P("row", "col"), P(), P(), P(), P()),
        out_specs=P("row", "col", None),
        check_vma=False,
    )
```

profile of v0, /device:TPU:7, one launch (start us, length us, event | category | flops | bytes accessed | tf_op | source)
XLA Modules:
  0.0 476.7 jit_solution(14973631442870226286)
XLA Ops:
  6.5 31.4 %all-gather = bf16[16,64,20]{1,2,0:T(8,128)(2,1)S(1)} all-gather(bf16[1,64,20]{1,2,0:T(8,128)(2,1)} %bitcast.47), channel_id=1, replica_groups=mesh['row'=16,'col'=32] {'row'}, dimensions={0}, use_global_device_ids=true | all-gather | bytes 43520 | tf_op jit(solution)/shard_map/all_gather | solution.py:29
  37.9 0.7 reshape.112
  38.7 0.8 dynamic_slice.12
  39.5 0.8 dynamic_slice.13
  40.2 0.1 broadcast_xor_fusion
  40.3 2.0 compare_select_fusion
  42.3 0.3 copy.37
  42.6 1.7 reshape.109
  44.3 72.5 %all-gather.4.cloned.1.call-done = bf16[32,20,1024]{2,1,0:T(8,128)(2,1)} async-done(((bf16[1,20,1024]{2,1,0:T(8,128)(2,1)}), bf16[32,20,1024]{2,1,0:T(8,128)(2,1)}) %all-gather.4.cloned.1.call-update) | async-done | bytes 1310736 | tf_op jit(solution)/shard_map/all_gather | solution.py:32
  116.8 2.3 reshape.114
  119.1 3.7 convolution_convert_fusion
  122.8 2.9 reshape.110
  125.7 14.8 %copy.40 = bf16[50,25,1024]{0,1,2:T(8,128)(2,1)} copy(bf16[50,25,1024]{2,1,0:T(8,128)(2,1)S(1)} %reshape.110) | data formatting | bytes 5120000 | tf_op jit(solution)/shard_map/reshape | solution.py:37
  140.5 16.4 %reshape.116 = bf16[16,2,40000]{2,1,0:T(2,128)(2,1)} reshape(bf16[1024,25,50]{2,1,0:T(8,128)(2,1)} %bitcast.41) | data formatting | bytes 5120000
  156.9 67.8 %all_to_all.54 = bf16[16,2,40000]{2,1,0:T(2,128)(2,1)} all-to-all(bf16[16,2,40000]{2,1,0:T(2,128)(2,1)} %reshape.116), channel_id=1, replica_groups=mesh['row'=16,'col'=32] {'row'}, dimensions={0} | all-to-all | bytes 5120000 | tf_op jit(solution)/shard_map/all_to_all | solution.py:38
  224.7 16.5 %reshape.117 = bf16[1024,25,50]{2,1,0:T(8,128)(2,1)} reshape(bf16[16,2,40000]{2,1,0:T(2,128)(2,1)} %all_to_all.54) | data formatting | bytes 5120000
  241.2 15.5 %copy.51 = bf16[16,50,25,64]{3,2,1,0:T(8,128)(2,1)} copy(bf16[16,50,25,64]{1,2,3,0:T(8,128)(2,1)} %bitcast.40) | data formatting | bytes 5120000 | tf_op jit(solution)/shard_map/all_to_all | solution.py:38
  256.7 8.7 %reshape.118 = bf16[32,2,20000]{2,1,0:T(2,128)(2,1)} reshape(bf16[800,25,64]{2,1,0:T(8,128)(2,1)} %bitcast.42) | data formatting | bytes 5120000
  265.4 69.3 %all_to_all.55 = bf16[32,2,20000]{2,1,0:T(2,128)(2,1)} all-to-all(bf16[32,2,20000]{2,1,0:T(2,128)(2,1)} %reshape.118), channel_id=1, replica_groups=mesh['row'=16,'col'=32] {'col'}, dimensions={0} | all-to-all | bytes 5120000 | tf_op jit(solution)/shard_map/all_to_all | solution.py:39
  334.7 9.9 %reshape.119 = bf16[800,25,64]{2,1,0:T(8,128)(2,1)} reshape(bf16[32,2,20000]{2,1,0:T(2,128)(2,1)} %all_to_all.55) | data formatting | bytes 5120000
  344.6 8.3 %copy.54 = bf16[25,32,25,64]{3,0,2,1:T(8,128)(2,1)} copy(bf16[25,32,25,64]{3,2,0,1:T(8,128)(2,1)} %bitcast.43) | data formatting | bytes 5120000 | tf_op jit(solution)/shard_map/all_to_all | solution.py:39
  352.9 12.9 %reshape.120 = bf16[16,2,40000]{2,1,0:T(2,128)(2,1)} reshape(bf16[800,25,64]{2,1,0:T(8,128)(2,1)} %bitcast.44) | data formatting | bytes 5120000
  365.8 7.1 %all-to-all-start.2 = ((bf16[16,2,40000]{2,1,0:T(2,128)(2,1)}), bf16[16,2,40000]{2,1,0:T(2,128)(2,1)}, u32[]{:S(2)}, u32[]{:S(2)}) async-start(bf16[16,2,40000]{2,1,0:T(2,128)(2,1)} %reshape.120), calls=%async_computation.2 | async-start | bytes 5128192 | tf_op jit(solution)/shard_map/all_to_all | solution.py:40
  372.9 0.8 dynamic_slice.14
  373.6 0.8 dynamic_slice.15
  374.4 0.1 broadcast_add_fusion
  374.5 0.1 add.82
  374.6 55.9 %all-to-all-done.2 = bf16[16,2,40000]{2,1,0:T(2,128)(2,1)} async-done(((bf16[16,2,40000]{2,1,0:T(2,128)(2,1)}), bf16[16,2,40000]{2,1,0:T(2,128)(2,1)}, u32[]{:S(2)}, u32[]{:S(2)}) %all-to-all-start.2) | async-done | bytes 2560032 | tf_op jit(solution)/shard_map/all_to_all | solution.py:40
  430.6 13.9 %reshape.121 = bf16[800,25,64]{2,1,0:T(8,128)(2,1)} reshape(bf16[16,2,40000]{2,1,0:T(2,128)(2,1)} %all-to-all-done.2) | data formatting | bytes 5120000
  444.5 8.6 %copy.48 = bf16[25,50,16,64]{3,2,1,0:T(8,128)(2,1)} copy(bf16[25,50,16,64]{3,0,1,2:T(8,128)(2,1)} %bitcast.45) | data formatting | bytes 5120000 | tf_op jit(solution)/shard_map/all_to_all | solution.py:40
  453.1 7.6 %all_to_all.50 = bf16[25,50,1024]{2,1,0:T(8,128)(2,1)} reshape(bf16[25,50,16,64]{3,2,1,0:T(8,128)(2,1)} %copy.48) | data formatting | bytes 5120000 | tf_op jit(solution)/shard_map/all_to_all | solution.py:40
  460.7 9.1 %fusion.1 = bf16[50,25,1024]{2,0,1:T(8,128)(2,1)} fusion(bf16[25,50,1024]{2,1,0:T(8,128)(2,1)} %all_to_all.50, bf16[50,25,1024]{2,1,0:T(8,128)(2,1)S(1)} %reshape.110, f32[1024]{0:T(1024)S(1)} %add.82, f32[50,25]{0,1:T(8,128)S(1)} %broadcast_add_fusion.1, s32[1024]{0:T(1024)S(1)} %fusion.14), kind=kOutput, calls=%fused_computation.2 | convolution fusion | flops 2628888576 | bytes 7693192 | tf_op jit(solution)/shard_map/bap,pq->abq/dot_general | solution.py:41
  (9 shorter events, 0.1 us)
Async XLA Ops:
  6.5 110.3 %all-gather.4.cloned.1.call-start = ((), (), s32[]{:S(2)}) async-start(), calls=%async_computation.3 | async-start | bytes 1622016 | tf_op jit(solution)/shard_map/all_gather | solution.py:32
  44.3 74.8 %copy-start = (bf16[1250,640]{1,0:T(8,128)(2,1)S(1)}, bf16[1250,640]{1,0:T(8,128)(2,1)}, u32[]{:S(2)}) copy-start(bf16[1250,640]{1,0:T(8,128)(2,1)} %reshape.109) | copy-start | bytes 4800004
  365.8 8.6 %copy-start.1 = (f32[32]{0:T(128)S(1)}, f32[32]{0:T(128)}, u32[]{:S(2)}) copy-start(f32[32]{0:T(128)} %param.11) | copy-start | bytes 388
  365.8 64.8 %all-to-all-start.2 = ((bf16[16,2,40000]{2,1,0:T(2,128)(2,1)}), bf16[16,2,40000]{2,1,0:T(2,128)(2,1)}, u32[]{:S(2)}, u32[]{:S(2)}) async-start(bf16[16,2,40000]{2,1,0:T(2,128)(2,1)} %reshape.120), calls=%async_computation.2 | async-start | bytes 5128192 | tf_op jit(solution)/shard_map/all_to_all | solution.py:40
Sparse Core Ops, SparseCore 0:
  38.8 77.9 all-gather.3
where the time goes:
time: 483 us; the launch traced here: 477 us
  blocking collectives  168 us (35%)
  local copies, waits for them, and re-layouts  144 us (30%)
  waiting for transfers between devices  128 us (27%)
  between operations  13.5 us (3%)
  matrix products  12.7 us (3%)
  starting transfers between devices  7.08 us (1%)
    unnamed x12, local copies, waits for them, and re-layouts  81.4 us
    all_gather x1, waiting for transfers between devices, per_device(): lax.all_gather(all_pairs, 'col', axis=1, tiled=True)  72.5 us
    all_to_all x1, blocking collectives, per_device(): lax.all_to_all(first_move, 'col', split_axis=0, concat_axis=1, tiled=True)  69.3 us
    all_to_all x1, blocking collectives, per_device(): lax.all_to_all(ladder, 'row', split_axis=2, concat_axis=0, tiled=True)  67.8 us
    all_to_all x1, waiting for transfers between devices, per_device(): lax.all_to_all(second_move, 'row', split_axis=1, concat_axis=2, tiled=True)  55.9 us
    all_gather x1, blocking collectives, per_device(): all_pairs = lax.all_gather(amplitudes, 'row', axis=0, tiled=True)  31.4 us
    reshape x2, local copies, waits for them, and re-layouts, per_device(): ladder = rounded.reshape(tile_a, tile_b, pairs)  17.7 us
    all_to_all x2, local copies, waits for them, and re-layouts, per_device(): lax.all_to_all(second_move, 'row', split_axis=1, concat_axis=2, tiled=True)  16.2 us
  transfers between devices with their start and end apart: 2, of which 2 were waited for; matrix products, arithmetic and copies ran while one was open for 2% of the time, Pallas kernels for 0%

commit v1 on v0

--- a/solution.py
+++ b/solution.py
@@ -1,7 +1,21 @@
+import functools
+
 import jax
 import jax.numpy as jnp
+import numpy as np
 from jax import lax
+from jax.experimental import pallas as pl
+from jax.experimental.pallas import tpu as pltpu
 from jax.sharding import PartitionSpec as P
+
+MESH = pl.DeviceIdType.MESH
+BF = jnp.bfloat16
+F32 = jnp.float32
+I32 = jnp.int32
+WIDE = 128
+PIECES = 8
+PIECE = 80
+DETOURS = ((0, 0), (1, 1), (3, 7), (2, 2), (2, 6), (3, 3), (1, 5), (0, 4))
 
 
 def pair_swapper(occupied):
@@ -11,7 +25,7 @@
     return (source[:, None] == target[None, :]).astype(jnp.bfloat16)
 
 
-def per_device(integrals, amplitudes, virt_irrep, pair_irrep, virt_energy, occ_energy):
+def long_runs(integrals, amplitudes, virt_irrep, pair_irrep, virt_energy, occ_energy):
     tile_a, tile_b, slab = integrals.shape
     occupied = occ_energy.shape[0]
     pairs = occupied * occupied
@@ -46,6 +60,549 @@
     return ((ladder.astype(jnp.float32) + other) / denom).astype(jnp.bfloat16)
 
 
+def chip_at(x, y, z, core):
+    return (
+        y * 2 + lax.div(x, 2),
+        lax.rem(x, 2) * 16 + z * 2 + core,
+    )
+
+
+def mirror_chip(x, y, z):
+    return (
+        lax.rem(z, 2) * 2 + lax.div(y, 4),
+        lax.rem(x, 2) * 4 + lax.div(z, 2),
+        lax.rem(y, 4) * 2 + lax.div(x, 2),
+    )
+
+
+def exchange_kernel(
+    virt_ref, energy_ref, occ_ref, pair_ref, amp_ref, g_ref,
+    t_out, c_out, r_out, ea_out, pe_out, info_ref, eb_ref,
+    gbuf, mbuf, stbuf, cf, cbuf, sendf, sbuf, mid, rbuf, blocks, tbuf, tile, tfull, eabuf, pebuf,
+    load_sem, out_sem, keep_sem,
+    s0_send, s0_recv, s1_send, s1_recv, ring_send, ring_recv, sib_send, sib_recv,
+    m1_send, m1_recv, m2_send, m2_recv,
+):
+    row = lax.axis_index("row")
+    col = lax.axis_index("col")
+    y, xh = lax.div(row, 2), lax.rem(row, 2)
+    xl, core = lax.div(col, 16), lax.rem(col, 2)
+    z = lax.div(lax.rem(col, 16), 2)
+    x = xh * 2 + xl
+    zq, z0 = lax.div(z, 2), lax.rem(z, 2)
+    straight = core == xl
+
+    load = pltpu.make_async_copy(g_ref, gbuf, load_sem)
+    load.start()
+
+    def remote(src, dst, send, recv, where):
+        return pltpu.make_async_remote_copy(
+            src_ref=src, dst_ref=dst, send_sem=send, recv_sem=recv,
+            device_id=where, device_id_type=MESH,
+        )
+
+    def near(d):
+        return chip_at(
+            lax.rem(x + 2 * (d // 4), 4), y,
+            zq * 2 + lax.rem(z0 + (d // 2) % 2, 2), lax.rem(core + d % 2, 2),
+        )
+
+    s1_x = jnp.where(straight, x, xh * 2 + 1 - xl)
+
+    def plane(d):
+        return chip_at(s1_x, y, lax.rem(z + 2 * d, 8), xl)
+
+    up = chip_at(x, lax.rem(y + 1, 8), z, core)
+    down = chip_at(x, lax.rem(y + 7, 8), z, core)
+    sibling = chip_at(x, y, z, 1 - core)
+    mx, my, mz = mirror_chip(x, y, z)
+
+    def ahead(t):
+        dx, dz = DETOURS[t]
+        return lax.rem(x + dx, 4), y, lax.rem(z + dz, 8)
+
+    def behind(t):
+        dx, dz = DETOURS[t]
+        return lax.rem(x + 4 - dx, 4), y, lax.rem(z + 8 - dz, 8)
+
+    def is_here(chip, k):
+        return (chip[0] == x) & (chip[1] == y) & (chip[2] == z) & (k == core)
+
+    targets = [mirror_chip(*behind(t)) for t in range(PIECES)]
+    feeders = [
+        (lax.rem(mx + DETOURS[t][0], 4), my, lax.rem(mz + DETOURS[t][1], 8))
+        for t in range(PIECES)
+    ]
+
+    barrier = pltpu.get_barrier_semaphore()
+
+    def greet(where):
+        pl.semaphore_signal(barrier, inc=1, device_id=where, device_id_type=MESH)
+
+    for t in range(PIECES):
+        for k in range(2):
+            @pl.when(jnp.logical_not(is_here(feeders[t], k)))
+            def _():
+                greet(chip_at(*feeders[t], k))
+    for t in range(1, PIECES):
+        greet(chip_at(*behind(t), core))
+    for d in range(1, 4):
+        greet(plane(d))
+
+    @pl.when(jnp.logical_not(straight))
+    def _():
+        greet(plane(0))
+
+    greet(up)
+    greet(down)
+    for d in range(1, 8):
+        greet(near(d))
+
+    a_at, b_at = row * 50, col * 25
+    la0, la1 = virt_ref[a_at], virt_ref[a_at + 49]
+    lb0, lb1 = virt_ref[b_at], virt_ref[b_at + 24]
+    sa = lax.fori_loop(0, 50, lambda i, n: n + jnp.where(virt_ref[a_at + i] == la0, 1, 0), jnp.int32(0))
+    sb = lax.fori_loop(0, 25, lambda i, n: n + jnp.where(virt_ref[b_at + i] == lb0, 1, 0), jnp.int32(0))
+
+    pair = pair_ref[...]
+    slab = pair.shape[1]
+    starts = [jnp.int32(0)]
+    for g in range(1, 8):
+        starts.append(jnp.sum(jnp.where(pair < g, 1.0, 0.0)).astype(I32))
+    ends = starts[1:] + [jnp.int32(slab)]
+    bases = [jnp.minimum(lax.div(s, 16) * 16, slab - WIDE) for s in starts]
+    base_of = jnp.zeros_like(pair)
+    fits = jnp.int32(1)
+    for g in range(8):
+        base_of = jnp.where(pair >= g, bases[g], base_of)
+        fits = jnp.where(ends[g] - bases[g] > WIDE, 0, fits)
+    slot_of = lax.broadcasted_iota(I32, pair.shape, 1) - base_of
+    stbuf[...] = jnp.where(
+        lax.broadcasted_iota(I32, (WIDE, slab), 0) == slot_of, 1.0, 0.0
+    ).astype(BF)
+
+    info_ref[0] = fits
+    info_ref[1] = sa
+    info_ref[2] = sb
+    for ja, la in enumerate((la0, la1)):
+        for jb, lb in enumerate((lb0, lb1)):
+            label = la ^ lb
+            base = jnp.int32(0)
+            for g in range(1, 8):
+                base = jnp.where(label == g, bases[g], base)
+            info_ref[4 + 2 * ja + jb] = base
+
+    amp = amp_ref[...].astype(F32)
+    packed = jnp.concatenate([amp[0:10], amp[10:20]], axis=1)
+    packed = jnp.concatenate([packed, jnp.zeros((6, 128), F32)], axis=0).astype(BF)
+    mine = xh * 4 + z0 * 2 + core
+    blocks[mine] = packed
+
+    mbuf[...] = jnp.zeros_like(mbuf)
+    load.wait()
+    first_part = lax.broadcasted_iota(I32, (50, slab), 0) < sa
+
+    def squeeze(i, carry):
+        for bb in range(5):
+            b = i * 5 + bb
+            lb = jnp.where(b < sb, lb0, lb1)
+            label = jnp.where(first_part, la0 ^ lb, la1 ^ lb)
+            tile = gbuf[b].astype(F32)
+            mbuf[bb, 0:50, :] = jnp.where(label == pair, tile, 0.0).astype(BF)
+        short = lax.dot_general(
+            mbuf[...].reshape(320, slab), stbuf[...], (((1,), (1,)), ((), ())),
+            preferred_element_type=F32,
+        )
+        at = pl.multiple_of(i * 320, 320)
+        cf[pl.ds(at, 320), :] = short
+        cbuf[pl.ds(at, 320), :] = short.astype(BF)
+        return carry
+
+    lax.fori_loop(0, 5, squeeze, 0)
+    for h in range(2):
+        sendf[h, 624:640, :] = jnp.zeros((16, 128), F32)
+        for i in range(25):
+            sendf[h, 25 * i:25 * i + 25, :] = cf[pl.ds(25 * h + i, 25, stride=64), :]
+        sbuf[h] = sendf[h].astype(BF).reshape(PIECES, PIECE, WIDE)
+
+    expected = jnp.where(straight, PIECES - 1 + 3 + 2 + 7, PIECES + 3 + 2 + 7)
+    for t in range(PIECES):
+        for k in range(2):
+            expected = expected + jnp.where(is_here(targets[t], k), 0, 1)
+    pl.semaphore_wait(barrier, expected)
+
+    near_copies = [
+        remote(blocks.at[mine], blocks.at[mine], s0_send.at[d - 1], s0_recv.at[mine], near(d))
+        for d in range(1, 8)
+    ]
+    for copy in near_copies:
+        copy.start()
+
+    def leg1(h, t):
+        return remote(
+            sbuf.at[h, t], mid.at[h, t], m1_send.at[h, t], m1_recv.at[h, t],
+            chip_at(*ahead(t), core),
+        )
+
+    def leg2(h, t, slot):
+        source = sbuf if t == 0 else mid
+        return remote(
+            source.at[h, t], rbuf.at[slot, t], m2_send.at[h, t], m2_recv.at[slot, t],
+            chip_at(*targets[t], h),
+        )
+
+    def keep_copy(h, t, slot):
+        source = sbuf if t == 0 else mid
+        return pltpu.make_async_copy(source.at[h, t], rbuf.at[slot, t], keep_sem.at[h, t])
+
+    def forward(h, t):
+        if t > 0:
+            leg1(h, t).wait_recv()
+        here = is_here(targets[t], h)
+
+        @pl.when(jnp.logical_not(here))
+        def _():
+            leg2(h, t, core).start()
+
+        @pl.when(here)
+        def _():
+            keep_copy(h, t, core).start()
+
+    for t in range(1, PIECES):
+        for h in range(2):
+            leg1(h, t).start()
+    for h in range(2):
+        forward(h, 0)
+
+    def near_arrived(s):
+        @pl.when(s != mine)
+        def _():
+            remote(blocks.at[s], blocks.at[s], s0_send.at[0], s0_recv.at[s], sibling).wait_recv()
+
+    for s in range(8):
+        near_arrived(s)
+    left = lax.broadcasted_iota(I32, (10, 128), 1) < 64
+    for q in range(4):
+        lo = blocks[q].astype(F32)[0:10]
+        hi = blocks[4 + q].astype(F32)[0:10]
+        tbuf[20 * q:20 * q + 10, :] = jnp.where(left, lo, pltpu.roll(hi, 64, 1))
+        tbuf[20 * q + 10:20 * q + 20, :] = jnp.where(left, pltpu.roll(lo, 64, 1), hi)
+
+    def part(half, quarter, yy):
+        at = pl.multiple_of(half * 320 + quarter * 80, 80)
+        return tfull.at[pl.ds(at, 80), pl.ds(pl.multiple_of(yy * 128, 128), 128)]
+
+    own_at = pl.multiple_of(xl * 320 + zq * 80, 80)
+    lane_at = pl.multiple_of(y * 128, 128)
+    tile[...] = tbuf[...].astype(BF)
+
+    @pl.when(straight)
+    def _():
+        tfull[pl.ds(own_at, 80), pl.ds(lane_at, 128)] = tile[...]
+
+    def spread(d):
+        return remote(
+            tile, part(xl, zq, y), s1_send.at[d], s1_recv.at[d], plane(d)
+        )
+
+    @pl.when(jnp.logical_not(straight))
+    def _():
+        spread(0).start()
+
+    for d in (1, 3, 2):
+        spread(d).start()
+
+    def ring(d, away, sign):
+        block = part(core, lax.rem(zq + 4 - d, 4), lax.rem(y + 8 - away * sign, 8))
+        index = away if sign > 0 else 8 - away
+        return index, block
+
+    def ring_copy(d, step, sign):
+        _, block = ring(d, step - 1, sign)
+        slot = 2 * step + (sign > 0) - 2
+        return remote(
+            block, block, ring_send.at[d, slot], ring_recv.at[d, slot],
+            up if sign > 0 else down,
+        )
+
+    def last_step(d, sign):
+        return 4 if (sign > 0) == (d < 2) else 3
+
+    def to_sibling(away, sign):
+        yy = lax.rem(y + 8 - away * sign, 8)
+        rows = pl.ds(pl.multiple_of(core * 320, 320), 320)
+        block = tfull.at[rows, pl.ds(pl.multiple_of(yy * 128, 128), 128)]
+        slot = away if sign > 0 else 8 - away
+        return remote(block, block, sib_send.at[slot], sib_recv.at[slot], sibling)
+
+    order = (0, 1, 3, 2)
+    for d in order:
+        if d == 0:
+            @pl.when(jnp.logical_not(straight))
+            def _():
+                spread(0).wait_recv()
+        else:
+            spread(d).wait_recv()
+        for sign in (1, -1):
+            ring_copy(d, 1, sign).start()
+    to_sibling(0, 1).start()
+
+    def around(step):
+        for d in order:
+            for sign in (1, -1):
+                if step <= last_step(d, sign):
+                    ring_copy(d, step, sign).wait_recv()
+                    if step + 1 <= last_step(d, sign):
+                        ring_copy(d, step + 1, sign).start()
+        for sign in (1, -1):
+            if step < 4 or sign > 0:
+                to_sibling(step, sign).start()
+
+    def deliver(ts):
+        for t in ts:
+            for h in range(2):
+                forward(h, t)
+
+    deliver((1, 2))
+    around(1)
+    deliver((3, 4))
+    around(2)
+    deliver((5, 6))
+    around(3)
+    deliver((7,))
+    around(4)
+
+    lane8 = lax.broadcasted_iota(I32, (8, 1024), 1)
+    first, second = lax.div(lane8, 32), lax.rem(lane8, 32)
+    pe = jnp.zeros((8, 1024), F32)
+    for i in range(32):
+        pe = pe + jnp.where(first == i, occ_ref[i], 0.0) + jnp.where(second == i, occ_ref[i], 0.0)
+    pebuf[...] = pe
+    sub = lax.broadcasted_iota(I32, (64, 128), 0)
+    ea = jnp.ones((64, 128), F32)
+    for i in range(50):
+        ea = jnp.where(sub == i, energy_ref[a_at + i], ea)
+    eabuf[...] = ea
+
+    def copy_eb(i, carry):
+        eb_ref[i] = energy_ref[b_at + i]
+        return carry
+
+    lax.fori_loop(0, 25, copy_eb, 0)
+
+    for slot in range(8):
+        step = slot if slot <= 4 else 8 - slot
+        to_sibling(step, 1 if slot <= 4 else -1).wait_recv()
+    outs = [
+        pltpu.make_async_copy(tfull, t_out, out_sem.at[0]),
+        pltpu.make_async_copy(cbuf, c_out, out_sem.at[1]),
+        pltpu.make_async_copy(eabuf, ea_out, out_sem.at[2]),
+        pltpu.make_async_copy(pebuf, pe_out, out_sem.at[3]),
+    ]
+    for copy in outs:
+        copy.start()
+    for t in range(PIECES):
+        here = [is_here(feeders[t], k) for k in range(2)]
+        for k in range(2):
+            @pl.when(jnp.logical_not(here[k]))
+            def _():
+                remote(
+                    mid.at[0, t], rbuf.at[k, t], m2_send.at[0, t], m2_recv.at[k, t], sibling
+                ).wait_recv()
+    for t in range(PIECES):
+        for h in range(2):
+            here = is_here(targets[t], h)
+
+            @pl.when(here)
+            def _():
+                keep_copy(h, t, core).wait()
+
+            @pl.when(jnp.logical_not(here))
+            def _():
+                leg2(h, t, core).wait_send()
+            if t > 0:
+                leg1(h, t).wait_send()
+    last = pltpu.make_async_copy(rbuf, r_out, out_sem.at[4])
+    last.start()
+    for copy in near_copies:
+        copy.wait_send()
+
+    @pl.when(jnp.logical_not(straight))
+    def _():
+        spread(0).wait_send()
+
+    for d in (1, 3, 2):
+        spread(d).wait_send()
+    for d in range(4):
+        for sign in (1, -1):
+            for step in range(1, last_step(d, sign) + 1):
+                ring_copy(d, step, sign).wait_send()
+    for slot in range(8):
+        step = slot if slot <= 4 else 8 - slot
+        to_sibling(step, 1 if slot <= 4 else -1).wait_send()
+    for copy in outs:
+        copy.wait()
+    last.wait()
+
+
+def exchange(g, amp, virt_irrep, pair_irrep, virt_energy, occ_energy):
+    dma, vmem = pltpu.SemaphoreType.DMA, pltpu.VMEM
+    smem_spec = pl.BlockSpec(memory_space=pltpu.SMEM)
+    vmem_spec = pl.BlockSpec(memory_space=pltpu.VMEM)
+    any_spec = pl.BlockSpec(memory_space=pl.ANY)
+    return pl.pallas_call(
+        exchange_kernel,
+        name="exchange",
+        out_shape=[
+            jax.ShapeDtypeStruct((640, 1024), BF),
+            jax.ShapeDtypeStruct((1600, WIDE), BF),
+            jax.ShapeDtypeStruct((2, PIECES, PIECE, WIDE), BF),
+            jax.ShapeDtypeStruct((64, 128), F32),
+            jax.ShapeDtypeStruct((8, 1024), F32),
+            jax.ShapeDtypeStruct((8,), I32),
+            jax.ShapeDtypeStruct((32,), F32),
+        ],
+        in_specs=[smem_spec, smem_spec, smem_spec, vmem_spec, vmem_spec, any_spec],
+        out_specs=[any_spec] * 5 + [smem_spec] * 2,
+        scratch_shapes=[
+            vmem((25, 50, 640), BF),
+            vmem((5, 64, 640), BF),
+            vmem((WIDE, 640), BF),
+            vmem((1600, WIDE), F32),
+            vmem((1600, WIDE), BF),
+            vmem((2, 640, WIDE), F32),
+            vmem((2, PIECES, PIECE, WIDE), BF),
+            vmem((2, PIECES, PIECE, WIDE), BF),
+            vmem((2, PIECES, PIECE, WIDE), BF),
+            vmem((8, 16, 128), BF),
+            vmem((80, 128), F32),
+            vmem((80, 128), BF),
+            vmem((640, 1024), BF),
+            vmem((64, 128), F32),
+            vmem((8, 1024), F32),
+            dma, dma((5,)), dma((2, PIECES)),
+            dma((7,)), dma((8,)), dma((4,)), dma((4,)), dma((4, 8)), dma((4, 8)),
+            dma((8,)), dma((8,)),
+            dma((2, PIECES)), dma((2, PIECES)), dma((2, PIECES)), dma((2, PIECES)),
+        ],
+        compiler_params=pltpu.CompilerParams(
+            collective_id=1, has_side_effects=True, vmem_limit_bytes=48 << 20
+        ),
+    )(virt_irrep, virt_energy, occ_energy, pair_irrep.reshape(1, -1), amp, g)
+
+
+def ladder_kernel(info, eb, c_ref, r_ref, t_ref, swap_ref, ea_ref, pe_ref, out_ref, xmf, xall, rhs, acc):
+    step = pl.program_id(0)
+    sa, sb = info[1], info[2]
+    two_a = sa < 50
+    two_b = sb < 25
+
+    @pl.when(step == 0)
+    def _():
+        xmf[...] = jnp.zeros_like(xmf)
+        for k in range(2):
+            block = r_ref[k].astype(F32)
+            for b in range(25):
+                xmf[64 * b + 25 * k:64 * b + 25 * k + 25, :] = block[25 * b:25 * b + 25]
+        xall[:, 0:WIDE] = c_ref[...]
+        xall[:, WIDE:2 * WIDE] = xmf[...].astype(BF)
+        for ja in range(2):
+            for jb in range(2):
+                def fill(ja=ja, jb=jb):
+                    base = pl.multiple_of(info[4 + 2 * ja + jb], 16)
+                    own = t_ref[pl.ds(base, WIDE), :]
+                    rhs[2 * ja + jb, 0:WIDE, :] = own
+                    rhs[2 * ja + jb, WIDE:2 * WIDE, :] = jnp.dot(
+                        own, swap_ref[...], preferred_element_type=F32
+                    ).astype(BF)
+
+                needed = True if ja + jb == 0 else (two_a if jb == 0 else two_b if ja == 0 else two_a & two_b)
+                if needed is True:
+                    fill()
+                else:
+                    pl.when(needed)(fill)
+
+    b0 = step * 5
+    at = pl.multiple_of(step * 320, 320)
+    place = lax.broadcasted_iota(I32, (320, 2 * WIDE), 0)
+    in_a = lax.rem(place, 64) >= sa
+    in_b = b0 + lax.div(place, 64) >= sb
+
+    def product(ja, jb):
+        side_a = in_a if ja else jnp.logical_not(in_a)
+        side_b = jnp.where(in_b, 1, 0) == jb
+        lhs = jnp.where(side_a & side_b, xall[pl.ds(at, 320), :].astype(F32), 0.0).astype(BF)
+        return jnp.dot(lhs, rhs[2 * ja + jb], preferred_element_type=F32)
+
+    lead = jnp.where(b0 >= sb, 1, 0)
+    straddle = (b0 < sb) & (b0 + 5 > sb)
+    acc[...] = product(0, lead)
+
+    @pl.when(two_a)
+    def _():
+        acc[...] += product(1, lead)
+
+    @pl.when(straddle)
+    def _():
+        acc[...] += product(0, 1)
+
+    @pl.when(straddle & two_a)
+    def _():
+        acc[...] += product(1, 1)
+
+    pe = pe_ref[0:1, :]
+    for bb in range(5):
+        ea = ea_ref[0:50, 0:1] + eb[b0 + bb]
+        out_ref[bb] = (acc[64 * bb:64 * bb + 50, :] / (ea - pe)).astype(BF)
+
+
+def ladder(t, c, r, ea, pe, info, eb, swap):
+    whole = lambda shape: pl.BlockSpec(shape, lambda i, *_: (0,) * len(shape))
+    return pl.pallas_call(
+        ladder_kernel,
+        name="ladder",
+        grid_spec=pltpu.PrefetchScalarGridSpec(
+            num_scalar_prefetch=2,
+            grid=(5,),
+            in_specs=[
+                whole((1600, WIDE)), whole((2, 640, WIDE)), whole((640, 1024)),
+                whole((1024, 1024)), whole((64, 128)), whole((8, 1024)),
+            ],
+            out_specs=pl.BlockSpec((5, 50, 1024), lambda i, *_: (i, 0, 0)),
+            scratch_shapes=[
+                pltpu.VMEM((1600, WIDE), F32),
+                pltpu.VMEM((1600, 2 * WIDE), BF),
+                pltpu.VMEM((4, 2 * WIDE, 1024), BF),
+                pltpu.VMEM((320, 1024), F32),
+            ],
+        ),
+        out_shape=jax.ShapeDtypeStruct((25, 50, 1024), BF),
+        compiler_params=pltpu.CompilerParams(vmem_limit_bytes=48 << 20),
+    )(info, eb, c, r.reshape(2, 640, WIDE), t, swap, ea, pe)
+
+
+def per_device(integrals, amplitudes, virt_irrep, pair_irrep, virt_energy, occ_energy):
+    g = jnp.transpose(integrals, (1, 0, 2))
+    t, c, r, ea, pe, info, eb = exchange(
+        g, amplitudes.T, virt_irrep, pair_irrep, virt_energy, occ_energy
+    )
+    source = np.arange(1024)
+    target = source % 32 * 32 + source // 32
+    swap = jnp.asarray((source[:, None] == target[None, :]).astype(jnp.bfloat16))
+
+    def short(_):
+        return ladder(t, c, r, ea, pe, info, eb, swap)
+
+    def general(_):
+        return jnp.transpose(
+            long_runs(integrals, amplitudes, virt_irrep, pair_irrep, virt_energy, occ_energy),
+            (1, 0, 2),
+        )
+
+    out = lax.cond(info[0] == 1, short, general, 0)
+    return jnp.transpose(out, (1, 0, 2))
+
+
 def solution(mesh):
     return jax.shard_map(
         per_device,

time: 483 us -> 79.3 us (0.16); the launches traced: 477 us -> 79 us
  blocking collectives: 168 us -> 0 us
  local copies, waits for them, and re-layouts: 144 us -> 2.28 us
  waiting for transfers between devices: 128 us -> 0 us
  Pallas kernels: 0 us -> 63.1 us
  matrix products: 12.7 us -> 0 us
  starting transfers between devices: 7.08 us -> 0 us
    all_to_all x2 -> x0, blocking collectives: 137 us -> none  [the longest x1 69.3 us: per_device(): lax.all_to_all(first_move, 'col', split_axis=0, concat_axis=1, tiled=True)]
    unnamed x12 -> x0, local copies, waits for them, and re-layouts: 81.4 us -> none
    all_gather x1 -> x0, waiting for transfers between devices: 72.5 us -> none  [per_device(): lax.all_gather(all_pairs, 'col', axis=1, tiled=True)]
    pallas_call x0 -> x2, Pallas kernels: none -> 63.1 us  [the longest x1 56.1 us: exchange(): pl.pallas_call(exchange_kernel, name='exchange', out_shape=[jax.ShapeDtyp...]
    all_to_all x1 -> x0, waiting for transfers between devices: 55.9 us -> none  [per_device(): lax.all_to_all(second_move, 'row', split_axis=1, concat_axis=2, tiled=True)]
    all_to_all x4 -> x0, local copies, waits for them, and re-layouts: 40 us -> none  [the longest x2 16.2 us: per_device(): lax.all_to_all(second_move, 'row', split_axis=1, concat_axis=2, tiled=True)]
    all_gather x1 -> x0, blocking collectives: 31.4 us -> none  [per_device(): all_pairs = lax.all_gather(amplitudes, 'row', axis=0, tiled=True)]
    reshape x3 -> x1, local copies, waits for them, and re-layouts: 19.4 us -> 0.69 us  [exchange(): pair_irrep.reshape(1, -1)]
  transfers between devices with their start and end apart: 2 -> 0, of which waited for: 2 -> 0; matrix products, arithmetic and copies ran while one was open for 2% -> 0% of each run, Pallas kernels for 0% -> 0%
where the time goes in v1:
time: 79.3 us; the launch traced here: 79 us
  Pallas kernels  63.1 us (80%)
  between operations  13.4 us (17%)
  local copies, waits for them, and re-layouts  2.28 us (3%)
    pallas_call x1, Pallas kernels, exchange(): pl.pallas_call(exchange_kernel, name='exchange', out_shape=[jax.ShapeDtyp...  56.1 us
    pallas_call x1, Pallas kernels, ladder(): pl.pallas_call(ladder_kernel, name='ladder', grid_spec=pltpu.PrefetchScal...  6.94 us
    cond x2, local copies, waits for them, and re-layouts  1.59 us

profile of v1, /device:TPU:7, one launch (start us, length us, event | category | flops | bytes accessed | tf_op | source)
XLA Modules:
  0.0 79.0 jit_solution(10068668860737902965)
XLA Ops:
  6.5 0.7 reshape.120.pair_ref
  7.2 56.1 %exchange.1 = (bf16[640,1024]{1,0:T(8,128)(2,1)}, bf16[1600,128]{1,0:T(8,128)(2,1)}, bf16[2,8,80,128]{3,2,1,0:T(8,128)(2,1)}, f32[64,128]{1,0:T(8,128)S(1)}, f32...) custom-call(s32[800]{0:T(1024)} %virt_ref.1, f32[800]{0:T(1024)} %energy_ref.1, f32[32]{0:T(128)} %occ_ref.1, ...), custom_call_target="tpu_custom_call" | custom-call | tf_op jit(solution)/shard_map/exchange/pallas_call | solution.py:453
  63.4 8.8 %conditional.1 = (bf16[25,50,1024]{2,1,0:T(8,128)(2,1)}) conditional(s32[]{:T(128)} %bitcast.20, (s32[800]{0:T(1024)}, s32[640]{0:T(1024)}, bf16[50,25,640]{2,0,1:T(8,128)(2,1)}, bf16[64,20]{0,1:T(8,128)(2,1)}, f32[800]{0:T(1024)}, /*index=5*/f32[32]{0:T(128)}) %tuple.11, (bf16[2,8,80,128]{3,2,1,0:T(8,128)(2,1)}, s32[8]{0:T(128)S(1)}, ...), branch_computations={%region_0.1_spmd, %region_1.2_spmd} | conditional | flops 4270186496 | bytes 112522960 | solution.py:602
  63.6 0.0 copy-start
  63.7 1.6 %copy-done = bf16[1024,1024]{1,0:T(8,128)(2,1)S(1)} copy-done((bf16[1024,1024]{1,0:T(8,128)(2,1)S(1)}, bf16[1024,1024]{1,0:T(8,128)(2,1)}, u32[]{:S(2)}) %copy-start) | copy-done | bytes 2097176 | tf_op jit(solution)/shard_map/cond
  65.2 6.9 %ladder.1 = bf16[25,50,1024]{2,1,0:T(8,128)(2,1)} custom-call(s32[8]{0:T(128)S(1)} %get-tuple-element.42.info, f32[32]{0:T(128)S(1)} %get-tuple-element.43.eb, bf16[1600,128]{1,0:T(8,128)(2,1)} %get-tuple-element.44.c_ref, bf16[2,640,128]{2,1,0:T(8,128)(2,1)} %bitcast.59, bf16[640,1024]{1,0:T(8,128)(2,1)} %get-tuple-element.46.t_ref, ...), custom_call_target="tpu_custom_call" | custom-call | tf_op jit(solution)/shard_map/cond/branch_1_fun/ladder/pallas_call | solution.py:561
Async XLA Ops:
  63.6 1.6 %copy-start = (bf16[1024,1024]{1,0:T(8,128)(2,1)S(1)}, bf16[1024,1024]{1,0:T(8,128)(2,1)}, u32[]{:S(2)}) copy-start(bf16[1024,1024]{1,0:T(8,128)(2,1)} %constant.55.clone.1.swap_ref) | copy-start | bytes 6291460 | tf_op jit(solution)/shard_map/cond

commit v2 on v1

--- a/solution.py
+++ b/solution.py
@@ -13,9 +13,10 @@
 F32 = jnp.float32
 I32 = jnp.int32
 WIDE = 128
-PIECES = 8
+RUN = 96
+PIECES = 6
 PIECE = 80
-DETOURS = ((0, 0), (1, 1), (3, 7), (2, 2), (2, 6), (3, 3), (1, 5), (0, 4))
+SPREAD = 8
 
 
 def pair_swapper(occupied):
@@ -76,10 +77,10 @@
 
 
 def exchange_kernel(
-    virt_ref, energy_ref, occ_ref, pair_ref, amp_ref, g_ref,
-    t_out, c_out, r_out, ea_out, pe_out, info_ref, eb_ref,
-    gbuf, mbuf, stbuf, cf, cbuf, sendf, sbuf, mid, rbuf, blocks, tbuf, tile, tfull, eabuf, pebuf,
-    load_sem, out_sem, keep_sem,
+    virt_ref, energy_ref, occ_ref, pair_ref, amp_ref, g_ref, swap_ref,
+    t_out, ts_out, c_out, r_out, ea_out, pe_out, info_ref, eb_ref,
+    gbuf, mbuf, stbuf, swapbuf, cf, cbuf, sendf, sbuf, mid, rbuf, blocks, tbuf, tile, tfull, tswap, eabuf, pebuf,
+    load_sem, swap_sem, out_sem, keep_sem,
     s0_send, s0_recv, s1_send, s1_recv, ring_send, ring_recv, sib_send, sib_recv,
     m1_send, m1_recv, m2_send, m2_recv,
 ):
@@ -94,6 +95,8 @@
 
     load = pltpu.make_async_copy(g_ref, gbuf, load_sem)
     load.start()
+    load_swap = pltpu.make_async_copy(swap_ref, swapbuf, swap_sem)
+    load_swap.start()
 
     def remote(src, dst, send, recv, where):
         return pltpu.make_async_remote_copy(
@@ -117,35 +120,36 @@
     sibling = chip_at(x, y, z, 1 - core)
     mx, my, mz = mirror_chip(x, y, z)
 
-    def ahead(t):
-        dx, dz = DETOURS[t]
-        return lax.rem(x + dx, 4), y, lax.rem(z + dz, 8)
-
-    def behind(t):
-        dx, dz = DETOURS[t]
-        return lax.rem(x + 4 - dx, 4), y, lax.rem(z + 8 - dz, 8)
+    def detour(k, h, t):
+        return lax.rem(4 * k + PIECES * h + t, SPREAD)
+
+    def ahead(d):
+        return lax.rem(x + d + 1, 4), y, lax.rem(z + d, 8)
+
+    def behind(d):
+        return lax.rem(x + 11 - d, 4), y, lax.rem(z + 8 - d, 8)
+
+    def beside_mirror(d):
+        return lax.rem(mx + d + 1, 4), my, lax.rem(mz + d, 8)
 
     def is_here(chip, k):
         return (chip[0] == x) & (chip[1] == y) & (chip[2] == z) & (k == core)
 
-    targets = [mirror_chip(*behind(t)) for t in range(PIECES)]
-    feeders = [
-        (lax.rem(mx + DETOURS[t][0], 4), my, lax.rem(mz + DETOURS[t][1], 8))
-        for t in range(PIECES)
-    ]
+    slots = [(h, t) for t in range(PIECES) for h in range(2)]
+    targets = {(h, t): mirror_chip(*behind(detour(core, h, t))) for h, t in slots}
+    feeders = {(k, t): beside_mirror(detour(k, core, t)) for k, t in slots}
 
     barrier = pltpu.get_barrier_semaphore()
 
     def greet(where):
         pl.semaphore_signal(barrier, inc=1, device_id=where, device_id_type=MESH)
 
-    for t in range(PIECES):
-        for k in range(2):
-            @pl.when(jnp.logical_not(is_here(feeders[t], k)))
-            def _():
-                greet(chip_at(*feeders[t], k))
-    for t in range(1, PIECES):
-        greet(chip_at(*behind(t), core))
+    for k, t in slots:
+        @pl.when(jnp.logical_not(is_here(feeders[k, t], k)))
+        def _():
+            greet(chip_at(*feeders[k, t], k))
+    for d in range(SPREAD):
+        greet(chip_at(*behind(d), core))
     for d in range(1, 4):
         greet(plane(d))
 
@@ -164,18 +168,17 @@
     sa = lax.fori_loop(0, 50, lambda i, n: n + jnp.where(virt_ref[a_at + i] == la0, 1, 0), jnp.int32(0))
     sb = lax.fori_loop(0, 25, lambda i, n: n + jnp.where(virt_ref[b_at + i] == lb0, 1, 0), jnp.int32(0))
 
-    pair = pair_ref[...]
-    slab = pair.shape[1]
+    slab = pair_ref.shape[0]
+    pair = pair_ref[...].reshape(1, slab)
     starts = [jnp.int32(0)]
     for g in range(1, 8):
         starts.append(jnp.sum(jnp.where(pair < g, 1.0, 0.0)).astype(I32))
     ends = starts[1:] + [jnp.int32(slab)]
-    bases = [jnp.minimum(lax.div(s, 16) * 16, slab - WIDE) for s in starts]
     base_of = jnp.zeros_like(pair)
     fits = jnp.int32(1)
     for g in range(8):
-        base_of = jnp.where(pair >= g, bases[g], base_of)
-        fits = jnp.where(ends[g] - bases[g] > WIDE, 0, fits)
+        base_of = jnp.where(pair >= g, starts[g], base_of)
+        fits = jnp.where(ends[g] - starts[g] > RUN, 0, fits)
     slot_of = lax.broadcasted_iota(I32, pair.shape, 1) - base_of
     stbuf[...] = jnp.where(
         lax.broadcasted_iota(I32, (WIDE, slab), 0) == slot_of, 1.0, 0.0
@@ -187,10 +190,10 @@
     for ja, la in enumerate((la0, la1)):
         for jb, lb in enumerate((lb0, lb1)):
             label = la ^ lb
-            base = jnp.int32(0)
+            start = jnp.int32(0)
             for g in range(1, 8):
-                base = jnp.where(label == g, bases[g], base)
-            info_ref[4 + 2 * ja + jb] = base
+                start = jnp.where(label == g, starts[g], start)
+            info_ref[4 + 2 * ja + jb] = start
 
     amp = amp_ref[...].astype(F32)
     packed = jnp.concatenate([amp[0:10], amp[10:20]], axis=1)
@@ -223,12 +226,20 @@
         sendf[h, 624:640, :] = jnp.zeros((16, 128), F32)
         for i in range(25):
             sendf[h, 25 * i:25 * i + 25, :] = cf[pl.ds(25 * h + i, 25, stride=64), :]
-        sbuf[h] = sendf[h].astype(BF).reshape(PIECES, PIECE, WIDE)
-
-    expected = jnp.where(straight, PIECES - 1 + 3 + 2 + 7, PIECES + 3 + 2 + 7)
-    for t in range(PIECES):
-        for k in range(2):
-            expected = expected + jnp.where(is_here(targets[t], k), 0, 1)
+        quarter = [sendf[h, 160 * i:160 * i + 160, :] for i in range(4)]
+        turned = [pltpu.roll(quarter[i], WIDE - 32 * i, 1) for i in range(1, 4)]
+        lane = lax.broadcasted_iota(I32, (160, WIDE), 1)
+        sheets = [
+            jnp.where(lane < 96, quarter[0], turned[0]),
+            jnp.where(lane < 64, turned[0], turned[1]),
+            jnp.where(lane < 32, turned[1], turned[2]),
+        ]
+        for i in range(3):
+            sbuf[h, 2 * i:2 * i + 2] = sheets[i].astype(BF).reshape(2, PIECE, WIDE)
+
+    expected = jnp.where(straight, SPREAD + 3 + 2 + 7, SPREAD + 4 + 2 + 7)
+    for h, t in slots:
+        expected = expected + jnp.where(is_here(targets[h, t], h), 0, 1)
     pl.semaphore_wait(barrier, expected)
 
     near_copies = [
@@ -241,38 +252,29 @@
     def leg1(h, t):
         return remote(
             sbuf.at[h, t], mid.at[h, t], m1_send.at[h, t], m1_recv.at[h, t],
-            chip_at(*ahead(t), core),
-        )
-
-    def leg2(h, t, slot):
-        source = sbuf if t == 0 else mid
+            chip_at(*ahead(detour(core, h, t)), core),
+        )
+
+    def leg2(h, t):
         return remote(
-            source.at[h, t], rbuf.at[slot, t], m2_send.at[h, t], m2_recv.at[slot, t],
-            chip_at(*targets[t], h),
-        )
-
-    def keep_copy(h, t, slot):
-        source = sbuf if t == 0 else mid
-        return pltpu.make_async_copy(source.at[h, t], rbuf.at[slot, t], keep_sem.at[h, t])
+            mid.at[h, t], rbuf.at[core, t], m2_send.at[h, t], m2_recv.at[core, t],
+            chip_at(*targets[h, t], h),
+        )
+
+    def keep_copy(h, t):
+        return pltpu.make_async_copy(mid.at[h, t], rbuf.at[core, t], keep_sem.at[h, t])
 
     def forward(h, t):
-        if t > 0:
-            leg1(h, t).wait_recv()
-        here = is_here(targets[t], h)
+        leg1(h, t).wait_recv()
+        here = is_here(targets[h, t], h)
 
         @pl.when(jnp.logical_not(here))
         def _():
-            leg2(h, t, core).start()
+            leg2(h, t).start()
 
         @pl.when(here)
         def _():
-            keep_copy(h, t, core).start()
-
-    for t in range(1, PIECES):
-        for h in range(2):
-            leg1(h, t).start()
-    for h in range(2):
-        forward(h, 0)
+            keep_copy(h, t).start()
 
     def near_arrived(s):
         @pl.when(s != mine)
@@ -363,13 +365,14 @@
             for h in range(2):
                 forward(h, t)
 
-    deliver((1, 2))
+    for h, t in slots:
+        leg1(h, t).start()
+
     around(1)
-    deliver((3, 4))
     around(2)
-    deliver((5, 6))
+    deliver((0, 1, 2))
     around(3)
-    deliver((7,))
+    deliver((3, 4, 5))
     around(4)
 
     lane8 = lax.broadcasted_iota(I32, (8, 1024), 1)
@@ -393,35 +396,43 @@
     for slot in range(8):
         step = slot if slot <= 4 else 8 - slot
         to_sibling(step, 1 if slot <= 4 else -1).wait_recv()
+    load_swap.wait()
+
+    def swapped(i, carry):
+        at = pl.multiple_of(i * 128, 128)
+        tswap[pl.ds(at, 128), :] = jnp.dot(
+            tfull[pl.ds(at, 128), :], swapbuf[...], preferred_element_type=F32
+        ).astype(BF)
+        return carry
+
+    lax.fori_loop(0, 5, swapped, 0)
     outs = [
         pltpu.make_async_copy(tfull, t_out, out_sem.at[0]),
+        pltpu.make_async_copy(tswap, ts_out, out_sem.at[5]),
         pltpu.make_async_copy(cbuf, c_out, out_sem.at[1]),
         pltpu.make_async_copy(eabuf, ea_out, out_sem.at[2]),
         pltpu.make_async_copy(pebuf, pe_out, out_sem.at[3]),
     ]
     for copy in outs:
         copy.start()
-    for t in range(PIECES):
-        here = [is_here(feeders[t], k) for k in range(2)]
-        for k in range(2):
-            @pl.when(jnp.logical_not(here[k]))
-            def _():
-                remote(
-                    mid.at[0, t], rbuf.at[k, t], m2_send.at[0, t], m2_recv.at[k, t], sibling
-                ).wait_recv()
-    for t in range(PIECES):
-        for h in range(2):
-            here = is_here(targets[t], h)
-
-            @pl.when(here)
-            def _():
-                keep_copy(h, t, core).wait()
-
-            @pl.when(jnp.logical_not(here))
-            def _():
-                leg2(h, t, core).wait_send()
-            if t > 0:
-                leg1(h, t).wait_send()
+    for k, t in slots:
+        @pl.when(jnp.logical_not(is_here(feeders[k, t], k)))
+        def _():
+            remote(
+                mid.at[0, t], rbuf.at[k, t], m2_send.at[0, t], m2_recv.at[k, t], sibling
+            ).wait_recv()
+    for h, t in slots:
+        here = is_here(targets[h, t], h)
+
+        @pl.when(here)
+        def _():
+            keep_copy(h, t).wait()
+
+        @pl.when(jnp.logical_not(here))
+        def _():
+            leg2(h, t).wait_send()
+
+        leg1(h, t).wait_send()
     last = pltpu.make_async_copy(rbuf, r_out, out_sem.at[4])
     last.start()
     for copy in near_copies:
@@ -445,7 +456,7 @@
     last.wait()
 
 
-def exchange(g, amp, virt_irrep, pair_irrep, virt_energy, occ_energy):
+def exchange(g, amp, virt_irrep, pair_irrep, virt_energy, occ_energy, swap):
     dma, vmem = pltpu.SemaphoreType.DMA, pltpu.VMEM
     smem_spec = pl.BlockSpec(memory_space=pltpu.SMEM)
     vmem_spec = pl.BlockSpec(memory_space=pltpu.VMEM)
@@ -455,6 +466,7 @@
         name="exchange",
         out_shape=[
             jax.ShapeDtypeStruct((640, 1024), BF),
+            jax.ShapeDtypeStruct((640, 1024), BF),
             jax.ShapeDtypeStruct((1600, WIDE), BF),
             jax.ShapeDtypeStruct((2, PIECES, PIECE, WIDE), BF),
             jax.ShapeDtypeStruct((64, 128), F32),
@@ -462,12 +474,13 @@
             jax.ShapeDtypeStruct((8,), I32),
             jax.ShapeDtypeStruct((32,), F32),
         ],
-        in_specs=[smem_spec, smem_spec, smem_spec, vmem_spec, vmem_spec, any_spec],
-        out_specs=[any_spec] * 5 + [smem_spec] * 2,
+        in_specs=[smem_spec, smem_spec, smem_spec, vmem_spec, vmem_spec, any_spec, any_spec],
+        out_specs=[any_spec] * 6 + [smem_spec] * 2,
         scratch_shapes=[
             vmem((25, 50, 640), BF),
             vmem((5, 64, 640), BF),
             vmem((WIDE, 640), BF),
+            vmem((1024, 1024), BF),
             vmem((1600, WIDE), F32),
             vmem((1600, WIDE), BF),
             vmem((2, 640, WIDE), F32),
@@ -478,43 +491,52 @@
             vmem((80, 128), F32),
             vmem((80, 128), BF),
             vmem((640, 1024), BF),
+            vmem((640, 1024), BF),
             vmem((64, 128), F32),
             vmem((8, 1024), F32),
-            dma, dma((5,)), dma((2, PIECES)),
+            dma, dma, dma((6,)), dma((2, PIECES)),
             dma((7,)), dma((8,)), dma((4,)), dma((4,)), dma((4, 8)), dma((4, 8)),
             dma((8,)), dma((8,)),
             dma((2, PIECES)), dma((2, PIECES)), dma((2, PIECES)), dma((2, PIECES)),
         ],
         compiler_params=pltpu.CompilerParams(
-            collective_id=1, has_side_effects=True, vmem_limit_bytes=48 << 20
+            collective_id=1, has_side_effects=True, vmem_limit_bytes=60 << 20
         ),
-    )(virt_irrep, virt_energy, occ_energy, pair_irrep.reshape(1, -1), amp, g)
-
-
-def ladder_kernel(info, eb, c_ref, r_ref, t_ref, swap_ref, ea_ref, pe_ref, out_ref, xmf, xall, rhs, acc):
+    )(virt_irrep, virt_energy, occ_energy, pair_irrep, amp, g, swap)
+
+
+def ladder_kernel(info, eb, c_ref, r_ref, t_ref, ts_ref, ea_ref, pe_ref, out_ref, messf, xall, rhs, acc):
     step = pl.program_id(0)
     sa, sb = info[1], info[2]
     two_a = sa < 50
     two_b = sb < 25
 
+    def base_of(ja, jb):
+        start = info[4 + 2 * ja + jb]
+        return pl.multiple_of(jnp.minimum(lax.div(start, 16) * 16, t_ref.shape[0] - WIDE), 16)
+
     @pl.when(step == 0)
     def _():
-        xmf[...] = jnp.zeros_like(xmf)
+        lane = lax.broadcasted_iota(I32, (160, WIDE), 1)
+        xall[:, 0:WIDE] = c_ref[...].astype(F32)
+        xall[:, WIDE:2 * WIDE] = jnp.zeros((1600, WIDE), F32)
         for k in range(2):
-            block = r_ref[k].astype(F32)
+            sheets = [r_ref[k, 160 * i:160 * i + 160, :].astype(F32) for i in range(3)]
+            messf[0:160, :] = jnp.where(lane < 96, sheets[0], 0.0)
+            for i in range(1, 4):
+                low = sheets[i] if i < 3 else jnp.zeros((160, WIDE), F32)
+                both = jnp.where(
+                    lane >= WIDE - 32 * i, sheets[i - 1], jnp.where(lane < 96 - 32 * i, low, 0.0)
+                )
+                messf[160 * i:160 * i + 160, :] = pltpu.roll(both, 32 * i, 1)
             for b in range(25):
-                xmf[64 * b + 25 * k:64 * b + 25 * k + 25, :] = block[25 * b:25 * b + 25]
-        xall[:, 0:WIDE] = c_ref[...]
-        xall[:, WIDE:2 * WIDE] = xmf[...].astype(BF)
+                xall[64 * b + 25 * k:64 * b + 25 * k + 25, WIDE:2 * WIDE] = messf[25 * b:25 * b + 25, :]
         for ja in range(2):
             for jb in range(2):
                 def fill(ja=ja, jb=jb):
-                    base = pl.multiple_of(info[4 + 2 * ja + jb], 16)
-                    own = t_ref[pl.ds(base, WIDE), :]
-                    rhs[2 * ja + jb, 0:WIDE, :] = own
-                    rhs[2 * ja + jb, WIDE:2 * WIDE, :] = jnp.dot(
-                        own, swap_ref[...], preferred_element_type=F32
-                    ).astype(BF)
+                    rows = pl.ds(base_of(ja, jb), WIDE)
+                    rhs[2 * ja + jb, 0:WIDE, :] = t_ref[rows, :]
+                    rhs[2 * ja + jb, WIDE:2 * WIDE, :] = ts_ref[rows, :]
 
                 needed = True if ja + jb == 0 else (two_a if jb == 0 else two_b if ja == 0 else two_a & two_b)
                 if needed is True:
@@ -524,14 +546,18 @@
 
     b0 = step * 5
     at = pl.multiple_of(step * 320, 320)
-    place = lax.broadcasted_iota(I32, (320, 2 * WIDE), 0)
+    place = lax.broadcasted_iota(I32, (320, WIDE), 0)
     in_a = lax.rem(place, 64) >= sa
     in_b = b0 + lax.div(place, 64) >= sb
 
     def product(ja, jb):
         side_a = in_a if ja else jnp.logical_not(in_a)
-        side_b = jnp.where(in_b, 1, 0) == jb
-        lhs = jnp.where(side_a & side_b, xall[pl.ds(at, 320), :].astype(F32), 0.0).astype(BF)
+        side = side_a & (jnp.where(in_b, 1, 0) == jb)
+        turn = info[4 + 2 * ja + jb] - base_of(ja, jb)
+        lhs = jnp.concatenate([
+            jnp.where(side, pltpu.roll(xall[pl.ds(at, 320), WIDE * i:WIDE * i + WIDE], turn, 1), 0.0).astype(BF)
+            for i in range(2)
+        ], axis=1)
         return jnp.dot(lhs, rhs[2 * ja + jb], preferred_element_type=F32)
 
     lead = jnp.where(b0 >= sb, 1, 0)
@@ -556,7 +582,7 @@
         out_ref[bb] = (acc[64 * bb:64 * bb + 50, :] / (ea - pe)).astype(BF)
 
 
-def ladder(t, c, r, ea, pe, info, eb, swap):
+def ladder(t, ts, c, r, ea, pe, info, eb):
     whole = lambda shape: pl.BlockSpec(shape, lambda i, *_: (0,) * len(shape))
     return pl.pallas_call(
         ladder_kernel,
@@ -565,33 +591,33 @@
             num_scalar_prefetch=2,
             grid=(5,),
             in_specs=[
-                whole((1600, WIDE)), whole((2, 640, WIDE)), whole((640, 1024)),
-                whole((1024, 1024)), whole((64, 128)), whole((8, 1024)),
+                whole((1600, WIDE)), whole((2, PIECES * PIECE, WIDE)), whole((640, 1024)),
+                whole((640, 1024)), whole((64, 128)), whole((8, 1024)),
             ],
             out_specs=pl.BlockSpec((5, 50, 1024), lambda i, *_: (i, 0, 0)),
             scratch_shapes=[
-                pltpu.VMEM((1600, WIDE), F32),
-                pltpu.VMEM((1600, 2 * WIDE), BF),
+                pltpu.VMEM((640, WIDE), F32),
+                pltpu.VMEM((1600, 2 * WIDE), F32),
                 pltpu.VMEM((4, 2 * WIDE, 1024), BF),
                 pltpu.VMEM((320, 1024), F32),
             ],
         ),
         out_shape=jax.ShapeDtypeStruct((25, 50, 1024), BF),
         compiler_params=pltpu.CompilerParams(vmem_limit_bytes=48 << 20),
-    )(info, eb, c, r.reshape(2, 640, WIDE), t, swap, ea, pe)
+    )(info, eb, c, r.reshape(2, PIECES * PIECE, WIDE), t, ts, ea, pe)
 
 
 def per_device(integrals, amplitudes, virt_irrep, pair_irrep, virt_energy, occ_energy):
     g = jnp.transpose(integrals, (1, 0, 2))
-    t, c, r, ea, pe, info, eb = exchange(
-        g, amplitudes.T, virt_irrep, pair_irrep, virt_energy, occ_energy
-    )
     source = np.arange(1024)
     target = source % 32 * 32 + source // 32
     swap = jnp.asarray((source[:, None] == target[None, :]).astype(jnp.bfloat16))
+    t, ts, c, r, ea, pe, info, eb = exchange(
+        g, amplitudes.T, virt_irrep, pair_irrep, virt_energy, occ_energy, swap
+    )
 
     def short(_):
-        return ladder(t, c, r, ea, pe, info, eb, swap)
+        return ladder(t, ts, c, r, ea, pe, info, eb)
 
     def general(_):
         return jnp.transpose(

time: 79.3 us -> 70.7 us (0.89)
  the two profiles are of different devices: /device:TPU:7 before, /device:TPU:75 now
where the time goes in v2:
time: 70.7 us; the launch traced here: 70.4 us
  Pallas kernels  56.8 us (80%)
  between operations  13.4 us (19%)
    pallas_call x1, Pallas kernels, exchange(): pl.pallas_call(exchange_kernel, name='exchange', out_shape=[jax.ShapeDtyp...  47.1 us
    pallas_call x1, Pallas kernels, ladder(): pl.pallas_call(ladder_kernel, name='ladder', grid_spec=pltpu.PrefetchScal...  9.7 us

profile of v2, /device:TPU:75, one launch (start us, length us, event | category | flops | bytes accessed | tf_op | source)
XLA Modules:
  0.0 70.4 jit_solution(1551002081208711636)
XLA Ops:
  6.5 0.0 copy-start.1
  6.5 0.0 copy-start.2
  6.5 47.1 %exchange.1 = (bf16[640,1024]{1,0:T(8,128)(2,1)}, bf16[640,1024]{1,0:T(8,128)(2,1)}, bf16[1600,128]{1,0:T(8,128)(2,1)}, bf16[2,6,80,128]{3,2,1,0:T(8,128)(2,1)S(...) custom-call(s32[800]{0:T(1024)} %virt_ref.1, f32[800]{0:T(1024)} %energy_ref.1, ...), custom_call_target="tpu_custom_call" | custom-call | tf_op jit(solution)/shard_map/exchange/pallas_call | solution.py:464
  53.6 0.0 copy-done.1
  53.7 0.0 copy-done.2
  53.7 9.9 %conditional.1 = (bf16[25,50,1024]{2,1,0:T(8,128)(2,1)}) conditional(s32[]{:T(128)} %bitcast.20, (s32[800]{0:T(1024)}, s32[640]{0:T(1024)S(1)}, bf16[50,25,640]{2,0,1:T(8,128)(2,1)}, bf16[64,20]{0,1:T(8,128)(2,1)S(1)}, f32[800]{0:T(1024)}, /*index=5*/f32[32]{0:T(128)}) %tuple.23, (bf16[2,6,80,128]{3,2,1,0:T(8,128)(2,1)S(1)}, s32[8]{0:T(128)S(1)}, ...), branch_computations={%region_0.1_spmd, %region_1.2_spmd} | conditional | flops 4270186496 | bytes 112522960 | solution.py:628
  53.9 9.7 %ladder.1 = bf16[25,50,1024]{2,1,0:T(8,128)(2,1)} custom-call(s32[8]{0:T(128)S(1)} %get-tuple-element.42.info, f32[32]{0:T(128)} %get-tuple-element.43.eb, bf16[1600,128]{1,0:T(8,128)(2,1)} %get-tuple-element.44.c_ref, bf16[2,480,128]{2,1,0:T(8,128)(2,1)S(1)} %bitcast.59, bf16[640,1024]{1,0:T(8,128)(2,1)} %get-tuple-element.46.t_ref, ...), custom_call_target="tpu_custom_call" | custom-call | tf_op jit(solution)/shard_map/cond/branch_1_fun/ladder/pallas_call | solution.py:587
Async XLA Ops:
  6.5 47.1 %copy-start.1 = (bf16[64,20]{0,1:T(8,128)(2,1)S(1)}, bf16[64,20]{0,1:T(8,128)(2,1)}, u32[]{:S(2)}) copy-start(bf16[64,20]{0,1:T(8,128)(2,1)} %param.10) | copy-start | bytes 7684
  6.5 47.1 %copy-start.2 = (s32[640]{0:T(1024)S(1)}, s32[640]{0:T(1024)}, u32[]{:S(2)}) copy-start(s32[640]{0:T(1024)} %pair_ref.1) | copy-start | bytes 7684

commit v3 on v2

--- a/solution.py
+++ b/solution.py
@@ -79,7 +79,7 @@
 def exchange_kernel(
     virt_ref, energy_ref, occ_ref, pair_ref, amp_ref, g_ref, swap_ref,
     t_out, ts_out, c_out, r_out, ea_out, pe_out, info_ref, eb_ref,
-    gbuf, mbuf, stbuf, swapbuf, cf, cbuf, sendf, sbuf, mid, rbuf, blocks, tbuf, tile, tfull, tswap, eabuf, pebuf,
+    gbuf, mbuf, stbuf, swapbuf, cf, cbuf, sendf, sbuf, mid, blocks, tbuf, tile, tfull, tswap, eabuf, pebuf,
     load_sem, swap_sem, out_sem, keep_sem,
     s0_send, s0_recv, s1_send, s1_recv, ring_send, ring_recv, sib_send, sib_recv,
     m1_send, m1_recv, m2_send, m2_recv,
@@ -237,11 +237,34 @@
         for i in range(3):
             sbuf[h, 2 * i:2 * i + 2] = sheets[i].astype(BF).reshape(2, PIECE, WIDE)
 
+    lane8 = lax.broadcasted_iota(I32, (8, 1024), 1)
+    first, second = lax.div(lane8, 32), lax.rem(lane8, 32)
+    pe = jnp.zeros((8, 1024), F32)
+    for i in range(32):
+        pe = pe + jnp.where(first == i, occ_ref[i], 0.0) + jnp.where(second == i, occ_ref[i], 0.0)
+    pebuf[...] = pe
+    sub = lax.broadcasted_iota(I32, (64, 128), 0)
+    ea = jnp.ones((64, 128), F32)
+    for i in range(50):
+        ea = jnp.where(sub == i, energy_ref[a_at + i], ea)
+    eabuf[...] = ea
+
+    def copy_eb(i, carry):
+        eb_ref[i] = energy_ref[b_at + i]
+        return carry
+
+    lax.fori_loop(0, 25, copy_eb, 0)
+
     expected = jnp.where(straight, SPREAD + 3 + 2 + 7, SPREAD + 4 + 2 + 7)
     for h, t in slots:
         expected = expected + jnp.where(is_here(targets[h, t], h), 0, 1)
     pl.semaphore_wait(barrier, expected)
 
+    outs = (
+        pltpu.make_async_copy(cbuf, c_out, out_sem.at[2, 0]),
+        pltpu.make_async_copy(eabuf, ea_out, out_sem.at[2, 1]),
+        pltpu.make_async_copy(pebuf, pe_out, out_sem.at[3, 0]),
+    )
     near_copies = [
         remote(blocks.at[mine], blocks.at[mine], s0_send.at[d - 1], s0_recv.at[mine], near(d))
         for d in range(1, 8)
@@ -257,12 +280,12 @@
 
     def leg2(h, t):
         return remote(
-            mid.at[h, t], rbuf.at[core, t], m2_send.at[h, t], m2_recv.at[core, t],
+            mid.at[h, t], r_out.at[core, t], m2_send.at[h, t], m2_recv.at[core, t],
             chip_at(*targets[h, t], h),
         )
 
     def keep_copy(h, t):
-        return pltpu.make_async_copy(mid.at[h, t], rbuf.at[core, t], keep_sem.at[h, t])
+        return pltpu.make_async_copy(mid.at[h, t], r_out.at[core, t], keep_sem.at[h, t])
 
     def forward(h, t):
         leg1(h, t).wait_recv()
@@ -368,6 +391,8 @@
     for h, t in slots:
         leg1(h, t).start()
 
+    for copy in outs:
+        copy.start()
     around(1)
     around(2)
     deliver((0, 1, 2))
@@ -375,51 +400,38 @@
     deliver((3, 4, 5))
     around(4)
 
-    lane8 = lax.broadcasted_iota(I32, (8, 1024), 1)
-    first, second = lax.div(lane8, 32), lax.rem(lane8, 32)
-    pe = jnp.zeros((8, 1024), F32)
-    for i in range(32):
-        pe = pe + jnp.where(first == i, occ_ref[i], 0.0) + jnp.where(second == i, occ_ref[i], 0.0)
-    pebuf[...] = pe
-    sub = lax.broadcasted_iota(I32, (64, 128), 0)
-    ea = jnp.ones((64, 128), F32)
-    for i in range(50):
-        ea = jnp.where(sub == i, energy_ref[a_at + i], ea)
-    eabuf[...] = ea
-
-    def copy_eb(i, carry):
-        eb_ref[i] = energy_ref[b_at + i]
-        return carry
-
-    lax.fori_loop(0, 25, copy_eb, 0)
-
+    load_swap.wait()
+
+    def rows_out(half):
+        rows = pl.ds(pl.multiple_of(half * 320, 320), 320)
+        return (
+            pltpu.make_async_copy(tfull.at[rows], t_out.at[rows], out_sem.at[0, half]),
+            pltpu.make_async_copy(tswap.at[rows], ts_out.at[rows], out_sem.at[1, half]),
+        )
+
+    def swapped(half):
+        rows = pl.ds(pl.multiple_of(half * 320, 320), 320)
+        plain, turned = rows_out(half)
+        plain.start()
+
+        def block(i, carry):
+            at = pl.ds(pl.multiple_of(half * 320 + i * 64, 64), 64)
+            tswap[at, :] = jnp.dot(tfull[at, :], swapbuf[...], preferred_element_type=F32).astype(BF)
+            return carry
+
+        lax.fori_loop(0, 5, block, 0)
+        turned.start()
+
+    swapped(core)
     for slot in range(8):
         step = slot if slot <= 4 else 8 - slot
         to_sibling(step, 1 if slot <= 4 else -1).wait_recv()
-    load_swap.wait()
-
-    def swapped(i, carry):
-        at = pl.multiple_of(i * 128, 128)
-        tswap[pl.ds(at, 128), :] = jnp.dot(
-            tfull[pl.ds(at, 128), :], swapbuf[...], preferred_element_type=F32
-        ).astype(BF)
-        return carry
-
-    lax.fori_loop(0, 5, swapped, 0)
-    outs = [
-        pltpu.make_async_copy(tfull, t_out, out_sem.at[0]),
-        pltpu.make_async_copy(tswap, ts_out, out_sem.at[5]),
-        pltpu.make_async_copy(cbuf, c_out, out_sem.at[1]),
-        pltpu.make_async_copy(eabuf, ea_out, out_sem.at[2]),
-        pltpu.make_async_copy(pebuf, pe_out, out_sem.at[3]),
-    ]
-    for copy in outs:
-        copy.start()
+    swapped(1 - core)
     for k, t in slots:
         @pl.when(jnp.logical_not(is_here(feeders[k, t], k)))
         def _():
             remote(
-                mid.at[0, t], rbuf.at[k, t], m2_send.at[0, t], m2_recv.at[k, t], sibling
+                mid.at[0, t], r_out.at[k, t], m2_send.at[0, t], m2_recv.at[k, t], sibling
             ).wait_recv()
     for h, t in slots:
         here = is_here(targets[h, t], h)
@@ -433,8 +445,6 @@
             leg2(h, t).wait_send()
 
         leg1(h, t).wait_send()
-    last = pltpu.make_async_copy(rbuf, r_out, out_sem.at[4])
-    last.start()
     for copy in near_copies:
         copy.wait_send()
 
@@ -451,9 +461,8 @@
     for slot in range(8):
         step = slot if slot <= 4 else 8 - slot
         to_sibling(step, 1 if slot <= 4 else -1).wait_send()
-    for copy in outs:
+    for copy in outs + rows_out(core) + rows_out(1 - core):
         copy.wait()
-    last.wait()
 
 
 def exchange(g, amp, virt_irrep, pair_irrep, virt_energy, occ_energy, swap):
@@ -486,7 +495,6 @@
             vmem((2, 640, WIDE), F32),
             vmem((2, PIECES, PIECE, WIDE), BF),
             vmem((2, PIECES, PIECE, WIDE), BF),
-            vmem((2, PIECES, PIECE, WIDE), BF),
             vmem((8, 16, 128), BF),
             vmem((80, 128), F32),
             vmem((80, 128), BF),
@@ -494,7 +502,7 @@
             vmem((640, 1024), BF),
             vmem((64, 128), F32),
             vmem((8, 1024), F32),
-            dma, dma, dma((6,)), dma((2, PIECES)),
+            dma, dma, dma((4, 2)), dma((2, PIECES)),
             dma((7,)), dma((8,)), dma((4,)), dma((4,)), dma((4, 8)), dma((4, 8)),
             dma((8,)), dma((8,)),
             dma((2, PIECES)), dma((2, PIECES)), dma((2, PIECES)), dma((2, PIECES)),

time: 70.7 us -> 70.5 us (level)
  the two profiles are of different devices: /device:TPU:75 before, /device:TPU:7 now
where the time goes in v3:
time: 70.5 us; the launch traced here: 70.1 us
  Pallas kernels  56.4 us (80%)
  between operations  13.4 us (19%)
    pallas_call x1, Pallas kernels, exchange(): pl.pallas_call(exchange_kernel, name='exchange', out_shape=[jax.ShapeDtyp...  47.6 us
    pallas_call x1, Pallas kernels, ladder(): pl.pallas_call(ladder_kernel, name='ladder', grid_spec=pltpu.PrefetchScal...  8.86 us

profile of v3, /device:TPU:7, one launch (start us, length us, event | category | flops | bytes accessed | tf_op | source)
XLA Modules:
  0.0 70.1 jit_solution(8815089524865201354)
XLA Ops:
  6.5 0.0 copy-start.1
  6.5 0.0 copy-start.2
  6.5 47.6 %exchange.1 = (bf16[640,1024]{1,0:T(8,128)(2,1)}, bf16[640,1024]{1,0:T(8,128)(2,1)}, bf16[1600,128]{1,0:T(8,128)(2,1)}, bf16[2,6,80,128]{3,2,1,0:T(8,128)(2,1)S(...) custom-call(s32[800]{0:T(1024)} %virt_ref.1, f32[800]{0:T(1024)} %energy_ref.1, ...), custom_call_target="tpu_custom_call" | custom-call | tf_op jit(solution)/shard_map/exchange/pallas_call | solution.py:473
  54.2 0.0 copy-done.1
  54.2 0.0 copy-done.2
  54.2 9.1 %conditional.1 = (bf16[25,50,1024]{2,1,0:T(8,128)(2,1)}) conditional(s32[]{:T(128)} %bitcast.20, (s32[800]{0:T(1024)}, s32[640]{0:T(1024)S(1)}, bf16[50,25,640]{2,0,1:T(8,128)(2,1)}, bf16[64,20]{0,1:T(8,128)(2,1)S(1)}, f32[800]{0:T(1024)}, /*index=5*/f32[32]{0:T(128)}) %tuple.23, (bf16[2,6,80,128]{3,2,1,0:T(8,128)(2,1)S(1)}, s32[8]{0:T(128)S(1)}, ...), branch_computations={%region_0.1_spmd, %region_1.2_spmd} | conditional | flops 4270186496 | bytes 112522960 | solution.py:636
  54.4 8.9 %ladder.1 = bf16[25,50,1024]{2,1,0:T(8,128)(2,1)} custom-call(s32[8]{0:T(128)S(1)} %get-tuple-element.42.info, f32[32]{0:T(128)} %get-tuple-element.43.eb, bf16[1600,128]{1,0:T(8,128)(2,1)} %get-tuple-element.44.c_ref, bf16[2,480,128]{2,1,0:T(8,128)(2,1)S(1)} %bitcast.59, bf16[640,1024]{1,0:T(8,128)(2,1)} %get-tuple-element.46.t_ref, ...), custom_call_target="tpu_custom_call" | custom-call | tf_op jit(solution)/shard_map/cond/branch_1_fun/ladder/pallas_call | solution.py:595
Async XLA Ops:
  6.5 47.6 %copy-start.1 = (bf16[64,20]{0,1:T(8,128)(2,1)S(1)}, bf16[64,20]{0,1:T(8,128)(2,1)}, u32[]{:S(2)}) copy-start(bf16[64,20]{0,1:T(8,128)(2,1)} %param.10) | copy-start | bytes 7684
  6.5 47.6 %copy-start.2 = (s32[640]{0:T(1024)S(1)}, s32[640]{0:T(1024)}, u32[]{:S(2)}) copy-start(s32[640]{0:T(1024)} %pair_ref.1) | copy-start | bytes 7684
